TPU v7x, 512 devices: a whole 4x4x16 slice. The times are simulated.
512 devices in a mesh: dp: 64 (over x, z), mp: 8 (over y, core).
Axes of the slice: x: 4, y: 4, z: 16, core: 2. Of those that a mesh axis runs over, the one named last changes fastest.
Arguments:
- queries: bfloat16 [32768, 2048], P('dp', 'mp'), may hold values from -6 to 6
- states: bfloat16 [256, 128, 448], P('dp', 'mp'), may hold values from -6 to 6
- gain: float32 [448], replicated, may hold values from 0.1 to 1.9
- w_kv: bfloat16 [2, 448, 2048], P(None, None, 'mp'), may hold values from -0.25 to 0.25
- neighbour_ids: int32 [512, 2], P('dp'), may hold values from 0 to 255, as said below
- block_place: int32 [256], replicated, may hold values from 0 to 255, as said below
- grad_out: bfloat16 [32768, 2048], P('dp', 'mp'), may hold values from -6 to 6
Outputs:
- attended: bfloat16 [32768, 2048], P('dp', 'mp')
- grad_queries: bfloat16 [32768, 2048], P('dp', 'mp')
- grad_kv: bfloat16 [2, 448, 2048], P(None, None, 'mp')
- grad_gain: float32 [448], replicated
Inputs may be any that keep to these rules, and one draw needn't show every extreme that they name: `neighbour_ids`: of the 16 ids named by the blocks of one dp index, at most 2 lie on any one owner (owner = block_place[id] // 4); one owner, the same for every dp index, holds exactly 2 of them for every dp index. `block_place`: A permutation of the ids.
All inputs are finite; a program needn't handle non-finite values.
Results may differ from a plain program's by a relative error of at most 0.015.
Values may be sent and summed in bfloat16 or wider, within the bound.
A program may use at most 64 MiB of HBM per device.

v0:
```python
import jax
import jax.numpy as jnp
from jax import lax
from jax.sharding import PartitionSpec as P

HD = 128
BLOCK = 64
NEIGH = 2
CAP = 2


def body(queries, states, gain, w_kv, neighbour_ids, block_place, grad_out):
    n_dp = lax.axis_size("dp")
    n_mp = lax.axis_size("mp")
    own_dev, slice_len, width_e = states.shape
    local_d = queries.shape[1]
    heads_here = local_d // HD
    units = neighbour_ids.shape[0]
    requests = units * NEIGH
    f32 = jnp.float32
    bf16 = jnp.bfloat16
    statef = states.astype(f32)
    normed = statef * lax.rsqrt(jnp.mean(statef * statef, -1, keepdims=True) + 1e-06)
    encoded = (normed * gain).astype(bf16)
    placed = jnp.take(block_place, neighbour_ids.reshape(-1))
    owner = placed // own_dev
    slot_id = placed % own_dev
    order = jnp.arange(requests)
    earlier = jnp.sum(
        (owner[:, None] == owner[None, :]) & (order[None, :] < order[:, None]), axis=1
    )
    bucket = owner * CAP + earlier
    buckets = n_dp * CAP
    pick = bucket[None, :] == jnp.arange(buckets)[:, None]
    pick_bf = pick.astype(bf16)
    slot_buf = (jnp.sum(jnp.where(pick, slot_id[None, :] + 1, 0), axis=1) - 1).reshape(n_dp, CAP)
    table = (
        lax.all_to_all(slot_buf, "dp", split_axis=0, concat_axis=0, tiled=True)[..., None]
        == jnp.arange(own_dev)
    ).astype(bf16)
    picked = jnp.einsum("pko,ose->pkse", table, encoded, preferred_element_type=f32).astype(bf16)
    arrived = lax.all_to_all(picked, "dp", split_axis=0, concat_axis=0, tiled=True)
    mine = jnp.einsum(
        "br,bse->rse",
        pick_bf,
        arrived.reshape(buckets, slice_len, width_e),
        preferred_element_type=f32,
    ).astype(bf16)
    neighbours = lax.all_gather(
        mine.reshape(requests * slice_len, width_e), "mp", axis=0, tiled=True
    )
    keys = jnp.dot(neighbours, w_kv[0], preferred_element_type=f32).astype(bf16)
    values = jnp.dot(neighbours, w_kv[1], preferred_element_type=f32).astype(bf16)
    span = NEIGH * slice_len

    def to_blocks(rows_in):
        grouped = rows_in.reshape(n_mp, units, span, local_d).transpose(1, 0, 2, 3)
        return grouped.reshape(units, n_mp * span, heads_here, HD)

    def from_blocks(per_block):
        grouped = per_block.reshape(units, n_mp, span, local_d).transpose(1, 0, 2, 3)
        return grouped.reshape(n_mp * units * span, local_d)

    key_c = to_blocks(keys)
    value_c = to_blocks(values)
    query_c = queries.reshape(units, BLOCK, heads_here, HD)
    grad_c = grad_out.reshape(units, BLOCK, heads_here, HD)
    scale = HD ** (-0.5)
    scores = jnp.einsum("uqhd,ukhd->uhqk", query_c, key_c, preferred_element_type=f32) * scale
    probs = jax.nn.softmax(scores, -1)
    probs_b = probs.astype(bf16)
    attended = jnp.einsum("uhqk,ukhd->uqhd", probs_b, value_c, preferred_element_type=f32).astype(
        bf16
    )
    d_probs = jnp.einsum("uqhd,ukhd->uhqk", grad_c, value_c, preferred_element_type=f32)
    delta = jnp.sum(d_probs * probs, -1, keepdims=True)
    d_scores = (probs * (d_probs - delta) * scale).astype(bf16)
    d_query = jnp.einsum("uhqk,ukhd->uqhd", d_scores, key_c, preferred_element_type=f32).astype(
        bf16
    )
    d_value = jnp.einsum("uhqk,uqhd->ukhd", probs_b, grad_c, preferred_element_type=f32).astype(
        bf16
    )
    d_key = jnp.einsum("uhqk,uqhd->ukhd", d_scores, query_c, preferred_element_type=f32).astype(
        bf16
    )
    d_key_rows = from_blocks(d_key)
    d_value_rows = from_blocks(d_value)
    weight_terms = jnp.stack(
        [
            jnp.einsum("re,rd->ed", neighbours, d_key_rows, preferred_element_type=f32),
            jnp.einsum("re,rd->ed", neighbours, d_value_rows, preferred_element_type=f32),
        ]
    )
    grad_kv = lax.psum(weight_terms, "dp").astype(bf16)
    dims = (((1,), (1,)), ((), ()))
    d_states = (
        lax.psum_scatter(
            (
                lax.dot_general(d_key_rows, w_kv[0], dims, preferred_element_type=f32)
                + lax.dot_general(d_value_rows, w_kv[1], dims, preferred_element_type=f32)
            ).astype(jnp.bfloat16),
            "mp",
            scatter_dimension=0,
            tiled=True,
        )
        .astype(jnp.float32)
        .astype(bf16)
    )
    grad_buf = (
        jnp.einsum(
            "br,rse->bse",
            pick_bf,
            d_states.reshape(requests, slice_len, width_e),
            preferred_element_type=f32,
        )
        .astype(bf16)
        .reshape(n_dp, CAP, slice_len, width_e)
    )
    returned, returned_slots = (
        lax.all_to_all(grad_buf, "dp", split_axis=0, concat_axis=0, tiled=True),
        lax.all_to_all(slot_buf, "dp", split_axis=0, concat_axis=0, tiled=True),
    )
    table = (returned_slots.reshape(-1)[:, None] == jnp.arange(own_dev)[None, :]).astype(bf16)
    d_encoded = jnp.einsum(
        "bo,bse->ose",
        table,
        returned.reshape(buckets, slice_len, width_e),
        preferred_element_type=f32,
    )
    grad_gain = lax.psum(jnp.sum(d_encoded * normed, axis=(0, 1)), ("dp", "mp"))
    return (
        attended.reshape(units * BLOCK, local_d),
        d_query.reshape(units * BLOCK, local_d),
        grad_kv,
        grad_gain,
    )


def solution(mesh):
    return jax.shard_map(
        body,
        mesh=mesh,
        in_specs=(
            P("dp", "mp"),
            P("dp", "mp", None),
            P(),
            P(None, None, "mp"),
            P("dp", None),
            P(),
            P("dp", "mp"),
        ),
        out_specs=(P("dp", "mp"), P("dp", "mp"), P(None, None, "mp"), P()),
        check_vma=False,
    )
```

profile of v0, /device:TPU:1, one launch (start us, length us, event | category | flops | bytes accessed | tf_op | source)
XLA Modules:
  0.0 752.9 jit_solution(2921978802700460063)
XLA Ops:
  9.9 19.1 %all-to-all-start = ((s32[64,1,2]{2,1,0:T(1,128)}), s32[64,1,2]{2,1,0:T(1,128)S(1)}, u32[]{:S(2)}, u32[]{:S(2)}) async-start(s32[64,1,2]{2,1,0:T(1,128)} %bitcast.2), calls=%async_computation | async-start | bytes 65536 | tf_op jit(solution)/shard_map/all_to_all | solution.py:38
  30.0 12.2 %all-to-all-done = s32[64,1,2]{2,1,0:T(1,128)S(1)} async-done(((s32[64,1,2]{2,1,0:T(1,128)}), s32[64,1,2]{2,1,0:T(1,128)S(1)}, u32[]{:S(2)}, u32[]{:S(2)}) %all-to-all-start) | async-done | bytes 544 | tf_op jit(solution)/shard_map/all_to_all | solution.py:38
  42.3 1.8 convolution_convert_fusion.2
  45.2 94.8 %all_to_all.17 = bf16[64,2,16,448]{3,2,1,0:T(8,128)(2,1)S(1)} all-to-all(bf16[64,2,16,448]{3,2,1,0:T(8,128)(2,1)S(1)} %copy.80), channel_id=1, replica_groups=mesh['dp'=64,'mp'=8] {'dp'}, dimensions={0} | all-to-all | bytes 3670016 | tf_op jit(solution)/shard_map/all_to_all | solution.py:42
  140.0 2.3 fusion.15
  144.3 33.2 %all-gather.2.cloned.1.call-done = bf16[2048,448]{1,0:T(8,128)(2,1)} async-done(((bf16[256,448]{1,0:T(8,128)(2,1)}), bf16[2048,448]{1,0:T(8,128)(2,1)}) %all-gather.2.cloned.1.call-update) | async-done | bytes 1835024 | tf_op jit(solution)/shard_map/all_gather | solution.py:49
  177.4 2.3 convolution_convert_fusion
  182.2 1.9 convolution_convert_fusion.1
  186.3 1.5 convolution_bitcast_fusion
  187.8 3.2 fusion.8
  191.0 8.5 %fusion.7 = bf16[8,256,2,128]{3,1,2,0:T(8,128)(2,1)S(1)} fusion(f32[8,2,64,256]{3,2,1,0:T(8,128)} %convolution_bitcast_fusion, bf16[8,64,2,128]{3,2,1,0:T(2,128)(2,1)S(1)} %reshape.235, f32[8,2,64,256]{3,2,1,0:T(8,128)} %get-tuple-element.7, f32[8,2,64]{2,1,0:T(2,128)S(1)} %get-tuple-element.6), kind=kOutput, calls=%fused_computation.15 | convolution fusion | flops 69469440 | bytes 3411968 | tf_op jit(solution)/shard_map/uhqk,uqhd->ukhd/dot_general | solution.py:84
  203.6 1.5 reshape.241
  205.1 1.4 copy.98
  207.2 1.9 add_convert_fusion
  209.2 39.1 %reduce-scatter.2.cloned.1.call-done = bf16[256,448]{0,1:T(8,128)(2,1)} async-done(((bf16[2048,448]{0,1:T(8,128)(2,1)}), bf16[256,448]{0,1:T(8,128)(2,1)}) %reduce-scatter.2.cloned.1.call-update) | async-done | bytes 229392 | tf_op jit(solution)/shard_map/reduce_scatter | solution.py:98
  249.3 2.1 convolution_convert_fusion.3
  251.5 4.5 copy.101
  256.0 14.6 %all-to-all-start.2 = ((bf16[64,2,16,448]{3,2,1,0:T(8,128)(2,1)}), bf16[64,2,16,448]{3,2,1,0:T(8,128)(2,1)}, u32[]{:S(2)}, u32[]{:S(2)}) async-start(bf16[64,2,16,448]{3,2,1,0:T(8,128)(2,1)} %bitcast.92), calls=%async_computation.3 | async-start | bytes 4194304 | tf_op jit(solution)/shard_map/all_to_all | solution.py:121
  272.0 8.1 %fusion.19 = bf16[8,64,2,128]{3,1,2,0:T(8,128)(2,1)S(1)} fusion(f32[8,2,64,256]{3,2,1,0:T(8,128)} %convolution_bitcast_fusion, bf16[8,256,2,128]{3,2,1,0:T(2,128)(2,1)} %copy-done.4, f32[8,2,64,256]{3,2,1,0:T(8,128)} %get-tuple-element.7, f32[8,2,64]{2,1,0:T(2,128)S(1)} %get-tuple-element.6), kind=kOutput, calls=%fused_computation.31 | convolution fusion | flops 69076224 | bytes 3411968 | tf_op jit(solution)/shard_map/uhqk,ukhd->uqhd/dot_general | solution.py:78
  281.1 3.5 fusion.18
  285.7 2.3 convolution_bitcast_fusion.1
  288.9 296.9 %all-reduce.1 = bf16[2,448,256]{2,1,0:T(8,128)(2,1)} all-reduce(f32[2,448,256]{2,1,0:T(8,128)S(1)} %pad_maximum_fusion), channel_id=1, replica_groups=mesh['dp'=64,'mp'=8] {'dp'}, use_global_device_ids=true, to_apply=%region_6.7 | all-reduce | flops 229376 | bytes 1376256 | tf_op jit(solution)/shard_map/psum | solution.py:95
  585.8 4.0 fusion.23
  589.7 156.3 %psum.15 = f32[448]{0:T(512)} all-reduce(f32[448]{0:T(512)S(1)} %fusion.23), channel_id=1, replica_groups=mesh['dp'=64,'mp'=8] {'dp','mp'}, use_global_device_ids=true, to_apply=%region_9.10 | all-reduce | flops 448 | bytes 3584 | tf_op jit(solution)/shard_map/psum | solution.py:131
  (71 shorter events, 21.5 us)
Async XLA Ops:
  7.2 1.0 copy-start
  9.9 32.3 %all-to-all-start = ((s32[64,1,2]{2,1,0:T(1,128)}), s32[64,1,2]{2,1,0:T(1,128)S(1)}, u32[]{:S(2)}, u32[]{:S(2)}) async-start(s32[64,1,2]{2,1,0:T(1,128)} %bitcast.2), calls=%async_computation | async-start | bytes 65536 | tf_op jit(solution)/shard_map/all_to_all | solution.py:38
  29.0 148.4 %all-gather.2.cloned.1.call-start = ((), (), s32[]{:S(2)}) async-start(), calls=%async_computation.4 | async-start | bytes 2359296 | tf_op jit(solution)/shard_map/all_gather | solution.py:49
  140.0 3.4 copy-start.11
  140.0 3.5 copy-start.12
  140.0 37.5 %copy-start.8 = (bf16[2,448,256]{2,1,0:T(8,128)(2,1)S(1)}, bf16[2,448,256]{2,1,0:T(8,128)(2,1)}, u32[]{:S(2)}) copy-start(bf16[2,448,256]{2,1,0:T(8,128)(2,1)} %param.10) | copy-start | bytes 1376260
  143.2 105.1 %reduce-scatter.2.cloned.1.call-start = ((), (), s32[]{:S(2)}) async-start(), calls=%async_computation.5 | async-start | bytes 2064384 | tf_op jit(solution)/shard_map/reduce_scatter | solution.py:98
  179.7 2.4 copy-start.1
  182.2 2.3 copy-start.4
  184.5 1.8 copy-start.5
  185.0 2.8 copy-start.3
  185.0 2.8 copy-start.6
  201.3 1.2 copy-start.7
  205.1 1.4 copy-start.9
  256.0 329.8 %all-to-all-start.2 = ((bf16[64,2,16,448]{3,2,1,0:T(8,128)(2,1)}), bf16[64,2,16,448]{3,2,1,0:T(8,128)(2,1)}, u32[]{:S(2)}, u32[]{:S(2)}) async-start(bf16[64,2,16,448]{3,2,1,0:T(8,128)(2,1)} %bitcast.92), calls=%async_computation.3 | async-start | bytes 4194304 | tf_op jit(solution)/shard_map/all_to_all | solution.py:121
  285.0 3.1 copy-start.2
  288.8 297.0 %copy-start.10 = (bf16[4,16,448]{2,1,0:T(8,128)(2,1)S(1)}, bf16[4,16,448]{2,1,0:T(8,128)(2,1)}, u32[]{:S(2)}) copy-start(bf16[4,16,448]{2,1,0:T(8,128)(2,1)} %param.8) | copy-start | bytes 172036
Sparse Core Ops, SparseCore 0:
  143.3 34.1 all-gather.1
  209.3 38.9 reduce-scatter.1
where the time goes:
time: 754 us; the launch traced here: 753 us
  blocking collectives  548 us (73%)
  waiting for transfers between devices  84.5 us (11%)
  matrix products  45.3 us (6%)
  starting transfers between devices  34 us (5%)
  local copies, waits for them, and re-layouts  23.3 us (3%)
  between operations  14.4 us (2%)
    psum x1, blocking collectives, body(): grad_kv = lax.psum(weight_terms, 'dp').astype(bf16)  297 us
    psum x1, blocking collectives, body(): grad_gain = lax.psum(jnp.sum(d_encoded * normed, axis=(0, 1)), ('dp', 'mp'))  156 us
    all_to_all x1, blocking collectives, body(): lax.all_to_all(picked, 'dp', split_axis=0, concat_axis=0, tiled=True)  94.8 us
    reduce_scatter x1, waiting for transfers between devices, body(): lax.psum_scatter((lax.dot_general(d_key_rows, w_kv[0], dims, preferred_el...  39.1 us
    all_gather x1, waiting for transfers between devices, body(): lax.all_gather(mine.reshape(requests * slice_len, width_e), 'mp', axis=0,...  33.2 us
    all_to_all x1, starting transfers between devices, body(): lax.all_to_all(slot_buf, 'dp', split_axis=0, concat_axis=0, tiled=True)  19.1 us
  transfers between devices with their start and end apart: 4, of which 3 were waited for; matrix products, arithmetic and copies ran while one was open for 3% of the time, Pallas kernels for 0%

commit v1 on v0

v1 whole, which is shorter than its diff:
```python
import functools

import jax
import jax.numpy as jnp
from jax import lax
from jax.experimental import pallas as pl
from jax.experimental.pallas import tpu as pltpu
from jax.sharding import PartitionSpec as P

HD = 128
BLOCK = 64
NEIGH = 2
NX, NY, NZ = 4, 4, 16
OWN = 4
UNITS = 8
REQ = 16
SLICE = 16
DE = 448
NMP = 8
PIECE = 32
NPIECE = DE // PIECE
QUARTERS = 4
QSLOTS = REQ // QUARTERS
F32 = jnp.float32
BF16 = jnp.bfloat16
MESH = pl.DeviceIdType.MESH


def dot(a, b, ca, cb):
    return lax.dot_general(a, b, (((ca,), (cb,)), ((), ())), preferred_element_type=F32)


def remote(src, dst, send, recv, to):
    return pltpu.make_async_remote_copy(
        src_ref=src, dst_ref=dst, send_sem=send, recv_sem=recv, device_id=to, device_id_type=MESH
    )


def kernel(
    states_hbm, gain_hbm, ids_hbm, place_hbm, w_hbm, q_hbm, g_hbm,
    out_ref, dq_ref, gkv_ref, ggain_ref,
    states_ref, gain_ref, ids_ref, place_ref, w_ref, q_ref, g_ref, load_sem,
    zbuf, idbuf, ids_s, out_x, from_x, nb,
    grad, xs, xr, acc, zs, rbuf, full, gm, gx, gz,
    id_send, id_recv, id_local, zr_send, zr_recv, zl_send, zl_recv,
    x_send, x_recv, y_send, y_recv, s_send, s_recv,
    rx_send, rx_recv, rz_send, rz_recv, gz_send, gz_recv, gx_send, gx_recv,
    m_send, m_recv, h_send, h_recv, v_send, v_recv,
):
    dp = lax.axis_index("dp")
    mp = lax.axis_index("mp")
    x, z, y, c = dp // NZ, dp % NZ, mp // 2, mp % 2
    to_z = lambda k: (x * NZ + (z + k + NZ) % NZ, mp)
    to_x = lambda k: ((x + k) % NX * NZ + z, mp)
    to_y = lambda k: (dp, (y + k) % NY * 2 + c)
    sib = (dp, y * 2 + 1 - c)
    sent = []

    def start(cp):
        cp.start()
        sent.append(cp)
        return cp

    loads = [
        pltpu.make_async_copy(src, dst, load_sem.at[i])
        for i, (src, dst) in enumerate(
            (
                (states_hbm, states_ref), (gain_hbm, gain_ref), (ids_hbm, ids_ref),
                (place_hbm, place_ref), (w_hbm, w_ref), (q_hbm, q_ref), (g_hbm, g_ref),
            )
        )
    ]
    for cp in loads:
        cp.start()

    barrier = pltpu.get_barrier_semaphore()
    near = [to_z(1), to_z(-1), to_z(2), to_z(-2), to_x(1), to_x(2), to_x(3), to_y(1), to_y(2), to_y(3), sib]
    for peer in near:
        pl.semaphore_signal(barrier, inc=1, device_id=peer, device_id_type=MESH)

    for cp in loads[:4]:
        cp.wait()
    own = states_ref[...].astype(F32)
    normed = own * lax.rsqrt(jnp.mean(own * own, -1, keepdims=True) + 1e-6)
    zbuf[pl.ds(z * OWN, OWN)] = (normed * gain_ref[...]).astype(BF16)
    lane = lax.broadcasted_iota(jnp.int32, (8, 128), 1)
    vec = jnp.zeros((8, 128), jnp.int32)
    for r in range(REQ):
        vec = jnp.where(lane == r, place_ref[ids_ref[r % NEIGH, r // NEIGH]], vec)
    idbuf[x] = vec

    pl.semaphore_wait(barrier, len(near))

    def z_copy(d, half, right):
        st = 1 if d == 1 else 2
        at = ((z - d + st + NZ) % NZ if right else (z + d - st) % NZ) * OWN + half * 2
        ref = zbuf.at[pl.ds(at, 2)]
        if right:
            return remote(ref, ref, zr_send.at[d - 1, half], zr_recv.at[d - 1, half], to_z(st))
        return remote(ref, ref, zl_send.at[d - 1, half], zl_recv.at[d - 1, half], to_z(-st))

    chains = [(True, 0), (False, 1), (True, 1), (False, 0)]
    reach = {(True, 0): 8, (True, 1): 7, (False, 0): 7, (False, 1): 8}
    live = {}
    for d in (2, 1):
        for right, half in chains:
            live[right, half, d] = start(z_copy(d, half, right))
    id_copies = [
        start(remote(idbuf.at[x], idbuf.at[x], id_send.at[k - 1], id_recv.at[k - 1], to_x(k)))
        for k in (2, 1, 3)
    ]
    for d in range(1, 9):
        for right, half in chains:
            n = reach[right, half]
            if d > n:
                continue
            live[right, half, d].wait_recv()
            if d + 2 <= n:
                live[right, half, d + 2] = start(z_copy(d + 2, half, right))
        if d == 2:
            for cp in id_copies:
                cp.wait_recv()
            local = pltpu.make_async_copy(idbuf, ids_s, id_local)
            local.start()
            local.wait()

    def wanted(who, r):
        p = ids_s[who, 0, r]
        return lax.rem(p, NZ * OWN), lax.div(p, NZ * OWN)

    x_copies = {}
    for j in range(QUARTERS):
        for k in (2, 1, 3):
            for r in range(j * QSLOTS, (j + 1) * QSLOTS):
                out_x[k - 1, r] = zbuf[wanted((x + k) % NX, r)[0]]
            slots = pl.ds(j * QSLOTS, QSLOTS)
            x_copies[k, j] = start(
                remote(
                    out_x.at[k - 1, slots], from_x.at[k - 1, slots],
                    x_send.at[k - 1, j], x_recv.at[k - 1, j], to_x(k),
                )
            )

    y_copies, s_copies = {}, {}

    def finish(j):
        for k in (1, 3, 2):
            x_copies[k, j].wait_recv()
        for r in range(j * QSLOTS, (j + 1) * QSLOTS):
            at, col = wanted(x, r)
            block = zbuf[at]
            for k in (1, 2, 3):
                block = jnp.where(col == (x + NX - k) % NX, from_x[k - 1, r], block)
            nb[mp, r] = block
        ref = nb.at[mp, pl.ds(j * QSLOTS, QSLOTS)]
        for k in (2, 1, 3):
            y_copies[k, j] = start(remote(ref, ref, y_send.at[k - 1, j], y_recv.at[k - 1, j], to_y(k)))
        s_copies[0, j] = start(remote(ref, ref, s_send.at[0, j], s_recv.at[0, j], sib))

    def relay(j):
        for k in (1, 3, 2):
            y_copies[k, j].wait_recv()
            ref = nb.at[(y + NY - k) % NY * 2 + c, pl.ds(j * QSLOTS, QSLOTS)]
            s_copies[k, j] = start(remote(ref, ref, s_send.at[k, j], s_recv.at[k, j], sib))

    scale = HD ** (-0.5)

    def attend(j):
        for k in range(4):
            s_copies[k, j].wait_recv()
        units = range(2 * j, 2 * j + 2)
        encs = [nb[:, NEIGH * u:NEIGH * (u + 1)].reshape(NMP * NEIGH * SLICE, DE) for u in units]
        keys = [dot(e, w_ref[0], 1, 0).astype(BF16) for e in encs]
        values = [dot(e, w_ref[1], 1, 0).astype(BF16) for e in encs]
        cells = []
        for i, u in enumerate(units):
            for h in range(2):
                rows, cols = slice(u * BLOCK, (u + 1) * BLOCK), slice(h * HD, (h + 1) * HD)
                cells.append((rows, cols, q_ref[rows, cols], g_ref[rows, cols], keys[i][:, cols], values[i][:, cols]))
        ss = [dot(q, k, 1, 1) * scale for _, _, q, g, k, v in cells]
        dps = [dot(g, v, 1, 1) for _, _, q, g, k, v in cells]
        es = [jnp.exp(s - jnp.max(s, -1, keepdims=True)) for s in ss]
        ps = [e / jnp.sum(e, -1, keepdims=True) for e in es]
        pbs = [p.astype(BF16) for p in ps]
        dss = [
            (p * (dp_ - jnp.sum(dp_ * p, -1, keepdims=True)) * scale).astype(BF16)
            for p, dp_ in zip(ps, dps)
        ]
        dks, dvs = [], []
        for (rows, cols, q, g, k, v), pb, ds in zip(cells, pbs, dss):
            out_ref[rows, cols] = dot(pb, v, 1, 0).astype(BF16)
            dq_ref[rows, cols] = dot(ds, k, 1, 0).astype(BF16)
            dks.append(dot(ds, q, 0, 0).astype(BF16))
            dvs.append(dot(pb, g, 0, 0).astype(BF16))
        enc = jnp.concatenate(encs, axis=0)
        dk = jnp.concatenate([jnp.concatenate(dks[0:2], axis=1), jnp.concatenate(dks[2:4], axis=1)], axis=0)
        dv = jnp.concatenate([jnp.concatenate(dvs[0:2], axis=1), jnp.concatenate(dvs[2:4], axis=1)], axis=0)
        for side, d in enumerate((dk, dv)):
            total = dot(enc, d, 0, 0)
            for h in range(2):
                part = total[:, h * HD:(h + 1) * HD]
                if j == 0:
                    grad[2 * side + h] = part
                else:
                    grad[2 * side + h] += part

    for step in range(QUARTERS + 2):
        if step < QUARTERS:
            finish(step)
        if 0 <= step - 1 < QUARTERS:
            relay(step - 1)
        if step == 2:
            for cp in loads[4:]:
                cp.wait()
        if 0 <= step - 2 < QUARTERS:
            attend(step - 2)

    HALF = DE // 2
    rx = {}
    for half in range(2):
        span = slice(half * HALF, (half + 1) * HALF)
        at = pl.ds(half * HALF, HALF)
        for k in (2, 1, 3):
            xs[k - 1, span] = grad[(x + k) % NX, span].astype(BF16)
            rx[k, half] = start(
                remote(xs.at[k - 1, at], xr.at[k - 1, at], rx_send.at[k - 1, half], rx_recv.at[k - 1, half], to_x(k))
            )

    prod = jnp.zeros((DE, HD), F32)
    for j in range(4):
        prod = prod + w_ref[j // 2, :, (j % 2) * HD:(j % 2 + 1) * HD].astype(F32) * grad[j]
    part = lax.dot_general(
        jnp.ones((8, HD), F32), prod, (((1,), (1,)), ((), ())),
        precision=lax.Precision.HIGHEST, preferred_element_type=F32,
    )[0:1] / gain_ref[...]
    tail = jnp.concatenate([part[:, 384:448], jnp.zeros((1, 64), F32)], axis=1)
    gm[mp] = jnp.concatenate(
        [part[:, 0:128], part[:, 128:256], part[:, 256:384], tail, jnp.zeros((4, 128), F32)], axis=0
    )
    m_copies = [
        start(remote(gm.at[mp], gm.at[mp], m_send.at[k - 1], m_recv.at[k - 1], (dp, (mp + k) % NMP)))
        for k in range(1, NMP)
    ]

    def rows_of(t):
        return pl.ds(pl.multiple_of((t // 2 + NPIECE // 2 * (t % 2)) * PIECE, PIECE), PIECE)

    def z_out(t):
        return remote(zs.at[rows_of(t)], rbuf.at[z], rz_send.at[t], rz_recv.at[z], (x * NZ + t, mp))

    def sum_x(half):
        for k in (1, 3, 2):
            rx[k, half].wait_recv()
        span = slice(half * HALF, (half + 1) * HALF)
        total = grad[x, span]
        for k in (1, 2, 3):
            total = total + xr[k - 1, span].astype(F32)
        acc[span] = total
        zs[span] = total.astype(BF16)
        for t in range(half, NPIECE, 2):
            pl.when(z != t)(z_out(t).start)

    sum_x(0)
    for cp in m_copies:
        cp.wait_recv()
    gx[x] = functools.reduce(lambda s, m: s + gm[m], range(1, NMP), gm[0])
    h_copies = [
        start(remote(gx.at[x], gx.at[x], h_send.at[k - 1], h_recv.at[k - 1], to_x(k))) for k in (2, 1, 3)
    ]
    sum_x(1)
    for cp in h_copies:
        cp.wait_recv()
    gz[z] = functools.reduce(lambda s, m: s + gx[m], range(1, NX), gx[0])
    v_copies = [
        start(remote(gz.at[z], gz.at[z], v_send.at[k - 1], v_recv.at[k - 1], to_z(k)))
        for k in range(1, NZ)
    ]

    def z_back(k):
        ref = full.at[x, rows_of(z)]
        return remote(ref, ref, gz_send.at[k - 1], gz_recv.at[z], to_z(k))

    @pl.when(z < NPIECE)
    def _():
        rbuf[z] = jnp.zeros((PIECE, HD), BF16)
        for s in range(NZ):
            arrival = remote(zs.at[rows_of(0)], rbuf.at[s], rz_send.at[s], rz_recv.at[s], to_z(1))
            pl.when(z != s)(arrival.wait_recv)
        total = acc[rows_of(z)]
        for s in range(NZ):
            total = total + rbuf[s].astype(F32)
        full[x, rows_of(z)] = total.astype(BF16)
        for k in range(1, NZ):
            z_back(k).start()

    back = {}
    for half in range(2):
        for t in range(half, NPIECE, 2):
            ref = full.at[x, rows_of(t)]
            pl.when(z != t)(remote(ref, ref, gz_send.at[0], gz_recv.at[t], to_z(1)).wait_recv)
        ref = full.at[x, pl.ds(half * HALF, HALF)]
        for k in (2, 1, 3):
            back[k, half] = start(remote(ref, ref, gx_send.at[k - 1, half], gx_recv.at[k - 1, half], to_x(k)))

    for cp in v_copies:
        cp.wait_recv()
    g = functools.reduce(lambda s, m: s + gz[m], range(1, NZ), gz[0])
    ggain_ref[...] = jnp.concatenate([g[0:1], g[1:2], g[2:3], g[3:4, 0:64]], axis=1)

    for cp in back.values():
        cp.wait_recv()
    for j in range(4):
        gkv_ref[j // 2, :, (j % 2) * HD:(j % 2 + 1) * HD] = full[j]

    for t in range(NPIECE):
        pl.when(z != t)(z_out(t).wait_send)

    @pl.when(z < NPIECE)
    def _():
        for k in range(1, NZ):
            z_back(k).wait_send()

    for cp in sent:
        cp.wait_send()


def body(queries, states, gain, w_kv, neighbour_ids, block_place, grad_out):
    dma = pltpu.SemaphoreType.DMA
    vmem = pltpu.VMEM
    block = (SLICE, DE)
    tok, cols = queries.shape
    any_spec = pl.BlockSpec(memory_space=pl.ANY)
    out_spec = pl.BlockSpec(memory_space=pltpu.VMEM)
    attended, d_query, grad_kv, grad_gain = pl.pallas_call(
        kernel,
        out_shape=(
            jax.ShapeDtypeStruct((tok, cols), BF16),
            jax.ShapeDtypeStruct((tok, cols), BF16),
            jax.ShapeDtypeStruct((2, DE, cols), BF16),
            jax.ShapeDtypeStruct((1, DE), F32),
        ),
        in_specs=[any_spec] * 7,
        out_specs=(out_spec,) * 4,
        scratch_shapes=[
            vmem(states.shape, BF16),
            vmem((1, DE), F32),
            pltpu.SMEM(neighbour_ids.shape[::-1], jnp.int32),
            pltpu.SMEM(block_place.shape, jnp.int32),
            vmem(w_kv.shape, BF16),
            vmem((tok, cols), BF16),
            vmem((tok, cols), BF16),
            dma((7,)),
            vmem((NZ * OWN,) + block, BF16),
            vmem((NX, 8, 128), jnp.int32),
            pltpu.SMEM((NX, 8, 128), jnp.int32),
            vmem((3, REQ) + block, BF16),
            vmem((3, REQ) + block, BF16),
            vmem((NMP, REQ) + block, BF16),
            vmem((4, DE, HD), F32),
            vmem((3, DE, HD), BF16),
            vmem((3, DE, HD), BF16),
            vmem((DE, HD), F32),
            vmem((DE, HD), BF16),
            vmem((NZ, PIECE, HD), BF16),
            vmem((NX, DE, HD), BF16),
            vmem((NMP, 8, 128), F32),
            vmem((NX, 8, 128), F32),
            vmem((NZ, 8, 128), F32),
            dma((3,)), dma((3,)), dma,
            dma((8, 2)), dma((8, 2)), dma((8, 2)), dma((8, 2)),
            dma((3, QUARTERS)), dma((3, QUARTERS)),
            dma((3, QUARTERS)), dma((3, QUARTERS)),
            dma((4, QUARTERS)), dma((4, QUARTERS)),
            dma((3, 2)), dma((3, 2)), dma((NZ,)), dma((NZ,)), dma((NZ,)), dma((NZ,)),
            dma((3, 2)), dma((3, 2)),
            dma((NMP,)), dma((NMP,)), dma((3,)), dma((3,)), dma((NZ,)), dma((NZ,)),
        ],
        compiler_params=pltpu.CompilerParams(
            collective_id=0, has_side_effects=True, vmem_limit_bytes=40 * 1024 * 1024
        ),
        name="retro_step",
    )(states, gain.reshape(1, DE), neighbour_ids.T, block_place, w_kv, queries, grad_out)
    return attended, d_query, grad_kv, grad_gain.reshape(DE)


def solution(mesh):
    return jax.shard_map(
        body,
        mesh=mesh,
        in_specs=(
            P("dp", "mp"),
            P("dp", "mp", None),
            P(),
            P(None, None, "mp"),
            P("dp", None),
            P(),
            P("dp", "mp"),
        ),
        out_specs=(P("dp", "mp"), P("dp", "mp"), P(None, None, "mp"), P()),
        check_vma=False,
    )
```

time: 754 us -> 101 us (0.13)
  blocking collectives: 548 us -> 0 us
  Pallas kernels: 0 us -> 91.6 us
  waiting for transfers between devices: 84.5 us -> 0 us
  matrix products: 45.3 us -> 0 us
  starting transfers between devices: 34 us -> 0 us
  local copies, waits for them, and re-layouts: 23.3 us -> 7.87 us
  between operations: 14.4 us -> 0.66 us
    psum x2 -> x0, blocking collectives: 453 us -> none  [the longest x1 297 us: body(): grad_kv = lax.psum(weight_terms, 'dp').astype(bf16)]
    all_to_all x1 -> x0, blocking collectives: 94.8 us -> none  [body(): lax.all_to_all(picked, 'dp', split_axis=0, concat_axis=0, tiled=True)]
    pallas_call x0 -> x1, Pallas kernels: none -> 91.6 us  [body(): pl.pallas_call(kernel, out_shape=(jax.ShapeDtypeStruct((tok, cols), BF16)...]
    dot_general x16 -> x0, matrix products: 45.3 us -> none  [the longest x1 8.49 us: body(): jnp.einsum('uhqk,uqhd->ukhd', d_scores, query_c, preferred_element_type=f32)]
    reduce_scatter x1 -> x0, waiting for transfers between devices: 39.1 us -> none  [body(): lax.psum_scatter((lax.dot_general(d_key_rows, w_kv[0], dims, preferred_el...]
    all_to_all x2 -> x0, starting transfers between devices: 33.7 us -> none  [the longest x1 19.1 us: body(): lax.all_to_all(slot_buf, 'dp', split_axis=0, concat_axis=0, tiled=True)]
    all_gather x1 -> x0, waiting for transfers between devices: 33.2 us -> none  [body(): lax.all_gather(mine.reshape(requests * slice_len, width_e), 'mp', axis=0,...]
    all_to_all x2 -> x0, waiting for transfers between devices: 12.2 us -> none  [the longest x1 12.2 us: body(): lax.all_to_all(slot_buf, 'dp', split_axis=0, concat_axis=0, tiled=True)]
  transfers between devices with their start and end apart: 4 -> 0, of which waited for: 3 -> 0; matrix products, arithmetic and copies ran while one was open for 3% -> 0% of each run, Pallas kernels for 0% -> 0%
where the time goes in v1:
time: 101 us; the launch traced here: 100 us
  Pallas kernels  91.6 us (91%)
  local copies, waits for them, and re-layouts  7.87 us (8%)
    pallas_call x1, Pallas kernels, body(): pl.pallas_call(kernel, out_shape=(jax.ShapeDtypeStruct((tok, cols), BF16)...  91.6 us
    unnamed x18, local copies, waits for them, and re-layouts  7.87 us

profile of v1, /device:TPU:1, one launch (start us, length us, event | category | flops | bytes accessed | tf_op | source)
XLA Modules:
  0.0 100.2 jit_solution(7658776346440324250)
XLA Ops:
  0.6 0.0 copy-start.4
  0.6 0.0 copy-start.5
  0.7 0.7 copy-done.4
  1.3 0.0 copy-done.5
  1.3 0.0 copy-start
  1.3 1.0 %copy-done = bf16[2,448,256]{2,1,0:T(8,128)(2,1)S(1)} copy-done((bf16[2,448,256]{2,1,0:T(8,128)(2,1)S(1)}, bf16[2,448,256]{2,1,0:T(8,128)(2,1)}, u32[]{:S(2)}) %copy-start) | copy-done | bytes 458776
  2.3 0.0 copy-start.1
  2.4 0.9 copy-done.1
  3.3 0.0 copy-start.2
  3.3 0.9 copy-done.2
  4.2 0.0 copy-start.3
  4.3 0.8 copy-done.3
  5.1 0.0 copy-start.6
  5.1 0.7 copy-done.6
  5.8 91.6 %retro_step.1 = (bf16[512,256]{1,0:T(8,128)(2,1)S(1)}, bf16[512,256]{1,0:T(8,128)(2,1)S(1)}, bf16[2,448,256]{2,1,0:T(8,128)(2,1)S(1)}, f32[1,448]{1,0:T(1,128)S(1)}) custom-call(bf16[4,16,448]{2,1,0:T(8,128)(2,1)S(1)} %copy-done.3, f32[1,448]{1,0:T(1,128)S(1)} %bitcast.3, s32[2,8]{1,0:T(2,128)S(1)} %bitcast.5, s32[256]{0:T(256)S(1)} %copy-done.6, ...), custom_call_target="tpu_custom_call" | custom-call | tf_op jit(solution)/shard_map/retro_step/pallas_call | solution.py:334
  97.4 0.7 copy.15
  98.1 0.7 copy.16
  98.8 0.8 copy.17
  99.6 0.6 copy.18
Async XLA Ops:
  0.6 0.7 copy-start.4
  0.6 0.7 copy-start.5
  1.3 1.0 %copy-start = (bf16[2,448,256]{2,1,0:T(8,128)(2,1)S(1)}, bf16[2,448,256]{2,1,0:T(8,128)(2,1)}, u32[]{:S(2)}) copy-start(bf16[2,448,256]{2,1,0:T(8,128)(2,1)} %w_hbm.1) | copy-start | bytes 1376260
  2.3 0.9 copy-start.1
  3.3 0.9 copy-start.2
  4.2 0.8 copy-start.3
  5.1 0.7 copy-start.6

commit v2 on v1

--- a/solution.py
+++ b/solution.py
@@ -16,10 +16,12 @@
 REQ = 16
 SLICE = 16
 DE = 448
+GAIN_PAD = 512
 NMP = 8
 PIECE = 32
 NPIECE = DE // PIECE
 QUARTERS = 4
+ZPARTS = 2
 QSLOTS = REQ // QUARTERS
 F32 = jnp.float32
 BF16 = jnp.bfloat16
@@ -38,8 +40,9 @@
 
 def kernel(
     states_hbm, gain_hbm, ids_hbm, place_hbm, w_hbm, q_hbm, g_hbm,
-    out_ref, dq_ref, gkv_ref, ggain_ref,
+    out_hbm, dq_hbm, gkv_hbm, ggain_ref,
     states_ref, gain_ref, ids_ref, place_ref, w_ref, q_ref, g_ref, load_sem,
+    out_ref, dq_ref, gkv_ref, store_sem,
     zbuf, idbuf, ids_s, out_x, from_x, nb,
     grad, xs, xr, acc, zs, rbuf, full, gm, gx, gz,
     id_send, id_recv, id_local, zr_send, zr_recv, zl_send, zl_recv,
@@ -91,38 +94,39 @@
 
     pl.semaphore_wait(barrier, len(near))
 
-    def z_copy(d, half, right):
-        st = 1 if d == 1 else 2
-        at = ((z - d + st + NZ) % NZ if right else (z + d - st) % NZ) * OWN + half * 2
-        ref = zbuf.at[pl.ds(at, 2)]
+    def z_copy(d, part, right):
+        st = 2 - d % 2
+        at = ((z - d + st + NZ) % NZ if right else (z + d - st) % NZ) * OWN + part * (OWN // ZPARTS)
+        ref = zbuf.at[pl.ds(at, OWN // ZPARTS)]
         if right:
-            return remote(ref, ref, zr_send.at[d - 1, half], zr_recv.at[d - 1, half], to_z(st))
-        return remote(ref, ref, zl_send.at[d - 1, half], zl_recv.at[d - 1, half], to_z(-st))
-
-    chains = [(True, 0), (False, 1), (True, 1), (False, 0)]
-    reach = {(True, 0): 8, (True, 1): 7, (False, 0): 7, (False, 1): 8}
+            return remote(ref, ref, zr_send.at[d - 1, part], zr_recv.at[d - 1, part], to_z(st))
+        return remote(ref, ref, zl_send.at[d - 1, part], zl_recv.at[d - 1, part], to_z(-st))
+
+    chains = [(right, part) for part in range(ZPARTS) for right in (True, False)]
+    reach = {(right, part): 8 if right == (part % 2 == 0) else 7 for right, part in chains}
     live = {}
     for d in (2, 1):
-        for right, half in chains:
-            live[right, half, d] = start(z_copy(d, half, right))
+        for right, part in chains:
+            live[right, part, d] = start(z_copy(d, part, right))
     id_copies = [
         start(remote(idbuf.at[x], idbuf.at[x], id_send.at[k - 1], id_recv.at[k - 1], to_x(k)))
         for k in (2, 1, 3)
     ]
-    for d in range(1, 9):
-        for right, half in chains:
-            n = reach[right, half]
-            if d > n:
-                continue
-            live[right, half, d].wait_recv()
-            if d + 2 <= n:
-                live[right, half, d + 2] = start(z_copy(d + 2, half, right))
+    for d in (2, 4, 6):
+        for right, part in chains:
+            live[right, part, d].wait_recv()
+            for e in (d + 2, d + 1):
+                if e <= reach[right, part]:
+                    live[right, part, e] = start(z_copy(e, part, right))
         if d == 2:
             for cp in id_copies:
                 cp.wait_recv()
             local = pltpu.make_async_copy(idbuf, ids_s, id_local)
             local.start()
             local.wait()
+    for (right, part, d), cp in live.items():
+        if d not in (2, 4, 6):
+            cp.wait_recv()
 
     def wanted(who, r):
         p = ids_s[who, 0, r]
@@ -215,6 +219,13 @@
         if 0 <= step - 2 < QUARTERS:
             attend(step - 2)
 
+    stores = [
+        pltpu.make_async_copy(out_ref, out_hbm, store_sem.at[0]),
+        pltpu.make_async_copy(dq_ref, dq_hbm, store_sem.at[1]),
+    ]
+    for cp in stores:
+        cp.start()
+
     HALF = DE // 2
     rx = {}
     for half in range(2):
@@ -233,10 +244,7 @@
         jnp.ones((8, HD), F32), prod, (((1,), (1,)), ((), ())),
         precision=lax.Precision.HIGHEST, preferred_element_type=F32,
     )[0:1] / gain_ref[...]
-    tail = jnp.concatenate([part[:, 384:448], jnp.zeros((1, 64), F32)], axis=1)
-    gm[mp] = jnp.concatenate(
-        [part[:, 0:128], part[:, 128:256], part[:, 256:384], tail, jnp.zeros((4, 128), F32)], axis=0
-    )
+    gm[mp] = jnp.concatenate([part, jnp.zeros((1, GAIN_PAD - DE), F32)], axis=1)
     m_copies = [
         start(remote(gm.at[mp], gm.at[mp], m_send.at[k - 1], m_recv.at[k - 1], (dp, (mp + k) % NMP)))
         for k in range(1, NMP)
@@ -305,12 +313,18 @@
     for cp in v_copies:
         cp.wait_recv()
     g = functools.reduce(lambda s, m: s + gz[m], range(1, NZ), gz[0])
-    ggain_ref[...] = jnp.concatenate([g[0:1], g[1:2], g[2:3], g[3:4, 0:64]], axis=1)
-
-    for cp in back.values():
-        cp.wait_recv()
-    for j in range(4):
-        gkv_ref[j // 2, :, (j % 2) * HD:(j % 2 + 1) * HD] = full[j]
+    ggain_ref[...] = g[:, :DE]
+
+    for half in range(2):
+        for k in (1, 3, 2):
+            back[k, half].wait_recv()
+        span = slice(half * HALF, (half + 1) * HALF)
+        for j in range(4):
+            gkv_ref[j // 2, span, (j % 2) * HD:(j % 2 + 1) * HD] = full[j, span]
+        at = pl.ds(half * HALF, HALF)
+        cp = pltpu.make_async_copy(gkv_ref.at[:, at], gkv_hbm.at[:, at], store_sem.at[2 + half])
+        cp.start()
+        stores.append(cp)
 
     for t in range(NPIECE):
         pl.when(z != t)(z_out(t).wait_send)
@@ -322,6 +336,36 @@
 
     for cp in sent:
         cp.wait_send()
+    for cp in stores:
+        cp.wait()
+
+
+def hand_over_kernel(*refs):
+    n = (len(refs) - 1) // 3
+    src, dst, held, sem = refs[:n], refs[n:2 * n], refs[2 * n:3 * n], refs[-1]
+    first = [pltpu.make_async_copy(src[i], held[i], sem.at[i]) for i in range(n)]
+    second = [pltpu.make_async_copy(held[i], dst[i], sem.at[n + i]) for i in range(n)]
+    for cp in first:
+        cp.start()
+    for a, b in zip(first, second):
+        a.wait()
+        b.start()
+    for cp in second:
+        cp.wait()
+
+
+def hand_over(results):
+    n = len(results)
+    hbm = pl.BlockSpec(memory_space=pltpu.HBM)
+    return pl.pallas_call(
+        hand_over_kernel,
+        out_shape=tuple(jax.ShapeDtypeStruct(r.shape, r.dtype) for r in results),
+        in_specs=[hbm] * n,
+        out_specs=(hbm,) * n,
+        scratch_shapes=[pltpu.VMEM(r.shape, r.dtype) for r in results] + [pltpu.SemaphoreType.DMA((2 * n,))],
+        compiler_params=pltpu.CompilerParams(vmem_limit_bytes=56 * 1024 * 1024),
+        name="hand_over",
+    )(*results)
 
 
 def body(queries, states, gain, w_kv, neighbour_ids, block_place, grad_out):
@@ -329,9 +373,9 @@
     vmem = pltpu.VMEM
     block = (SLICE, DE)
     tok, cols = queries.shape
-    any_spec = pl.BlockSpec(memory_space=pl.ANY)
+    hbm = pl.BlockSpec(memory_space=pltpu.HBM)
     out_spec = pl.BlockSpec(memory_space=pltpu.VMEM)
-    attended, d_query, grad_kv, grad_gain = pl.pallas_call(
+    results = pl.pallas_call(
         kernel,
         out_shape=(
             jax.ShapeDtypeStruct((tok, cols), BF16),
@@ -339,8 +383,8 @@
             jax.ShapeDtypeStruct((2, DE, cols), BF16),
             jax.ShapeDtypeStruct((1, DE), F32),
         ),
-        in_specs=[any_spec] * 7,
-        out_specs=(out_spec,) * 4,
+        in_specs=[hbm] * 7,
+        out_specs=(hbm,) * 3 + (out_spec,),
         scratch_shapes=[
             vmem(states.shape, BF16),
             vmem((1, DE), F32),
@@ -350,6 +394,10 @@
             vmem((tok, cols), BF16),
             vmem((tok, cols), BF16),
             dma((7,)),
+            vmem((tok, cols), BF16),
+            vmem((tok, cols), BF16),
+            vmem(w_kv.shape, BF16),
+            dma((4,)),
             vmem((NZ * OWN,) + block, BF16),
             vmem((NX, 8, 128), jnp.int32),
             pltpu.SMEM((NX, 8, 128), jnp.int32),
@@ -363,11 +411,11 @@
             vmem((DE, HD), BF16),
             vmem((NZ, PIECE, HD), BF16),
             vmem((NX, DE, HD), BF16),
-            vmem((NMP, 8, 128), F32),
-            vmem((NX, 8, 128), F32),
-            vmem((NZ, 8, 128), F32),
+            vmem((NMP, 1, GAIN_PAD), F32),
+            vmem((NX, 1, GAIN_PAD), F32),
+            vmem((NZ, 1, GAIN_PAD), F32),
             dma((3,)), dma((3,)), dma,
-            dma((8, 2)), dma((8, 2)), dma((8, 2)), dma((8, 2)),
+            dma((8, ZPARTS)), dma((8, ZPARTS)), dma((8, ZPARTS)), dma((8, ZPARTS)),
             dma((3, QUARTERS)), dma((3, QUARTERS)),
             dma((3, QUARTERS)), dma((3, QUARTERS)),
             dma((4, QUARTERS)), dma((4, QUARTERS)),
@@ -376,10 +424,11 @@
             dma((NMP,)), dma((NMP,)), dma((3,)), dma((3,)), dma((NZ,)), dma((NZ,)),
         ],
         compiler_params=pltpu.CompilerParams(
-            collective_id=0, has_side_effects=True, vmem_limit_bytes=40 * 1024 * 1024
+            collective_id=0, has_side_effects=True, vmem_limit_bytes=56 * 1024 * 1024
         ),
         name="retro_step",
     )(states, gain.reshape(1, DE), neighbour_ids.T, block_place, w_kv, queries, grad_out)
+    attended, d_query, grad_kv, grad_gain = hand_over(results)
     return attended, d_query, grad_kv, grad_gain.reshape(DE)
 
 

time: 101 us -> 89.7 us (0.89)
  local copies, waits for them, and re-layouts: 7.87 us -> 0 us
  Pallas kernels: 91.6 us -> 88.9 us
    unnamed x18 -> x0, local copies, waits for them, and re-layouts: 7.87 us -> none
    pallas_call x1, Pallas kernels: 91.6 us -> 86.9 us  [body(): pl.pallas_call(kernel, out_shape=(jax.ShapeDtypeStruct((tok, cols), BF16)...]
    pallas_call x0 -> x1, Pallas kernels: none -> 2.02 us  [hand_over(): pl.pallas_call(hand_over_kernel, out_shape=tuple((jax.ShapeDtypeStruct(r....]
where the time goes in v2:
time: 89.7 us; the launch traced here: 89.5 us
  Pallas kernels  88.9 us (99%)
    pallas_call x1, Pallas kernels, body(): pl.pallas_call(kernel, out_shape=(jax.ShapeDtypeStruct((tok, cols), BF16)...  86.9 us
    pallas_call x1, Pallas kernels, hand_over(): pl.pallas_call(hand_over_kernel, out_shape=tuple((jax.ShapeDtypeStruct(r....  2.02 us

profile of v2, /device:TPU:1, one launch (start us, length us, event | category | flops | bytes accessed | tf_op | source)
XLA Modules:
  0.0 89.5 jit_solution(5984963923126140448)
XLA Ops:
  0.6 86.9 %retro_step.1 = (bf16[512,256]{1,0:T(8,128)(2,1)}, bf16[512,256]{1,0:T(8,128)(2,1)}, bf16[2,448,256]{2,1,0:T(8,128)(2,1)}, f32[1,448]{1,0:T(1,128)}) custom-call(bf16[4,16,448]{2,1,0:T(8,128)(2,1)} %states_hbm.1, f32[1,448]{1,0:T(1,128)} %bitcast.3, s32[2,8]{1,0:T(2,128)} %bitcast.4, s32[256]{0:T(256)} %place_hbm.1, bf16[2,448,256]{2,1,0:T(8,128)(2,1)} %w_hbm.1, ...), custom_call_target="tpu_custom_call" | custom-call | tf_op jit(solution)/shard_map/retro_step/pallas_call | solution.py:378
  87.5 2.0 %hand_over.1 = (bf16[512,256]{1,0:T(8,128)(2,1)}, bf16[512,256]{1,0:T(8,128)(2,1)}, bf16[2,448,256]{2,1,0:T(8,128)(2,1)}, f32[1,448]{1,0:T(1,128)}) custom-call(bf16[512,256]{1,0:T(8,128)(2,1)} %get-tuple-element.12.refs_0_, bf16[512,256]{1,0:T(8,128)(2,1)} %get-tuple-element.13.refs_1_, bf16[2,448,256]{2,1,0:T(8,128)(2,1)} %get-tuple-element.14.refs_2_, ...), custom_call_target="tpu_custom_call" | custom-call | tf_op jit(solution)/shard_map/hand_over/pallas_call | solution.py:360

commit v3 on v2

--- a/solution.py
+++ b/solution.py
@@ -20,9 +20,12 @@
 NMP = 8
 PIECE = 32
 NPIECE = DE // PIECE
-QUARTERS = 4
-ZPARTS = 2
-QSLOTS = REQ // QUARTERS
+PAIRS = REQ // 2
+TILES = 7
+WINDOW = 2
+LAG = 3
+GROUPS = {7: ((0, 1, 2, 3),), 10: ((4, 5, 6, 7),)}
+LANES = 128
 F32 = jnp.float32
 BF16 = jnp.bfloat16
 MESH = pl.DeviceIdType.MESH
@@ -44,7 +47,7 @@
     states_ref, gain_ref, ids_ref, place_ref, w_ref, q_ref, g_ref, load_sem,
     out_ref, dq_ref, gkv_ref, store_sem,
     zbuf, idbuf, ids_s, out_x, from_x, nb,
-    grad, xs, xr, acc, zs, rbuf, full, gm, gx, gz,
+    grad, xs, xr, acc, zs, rbuf, gm, gx, gz,
     id_send, id_recv, id_local, zr_send, zr_recv, zl_send, zl_recv,
     x_send, x_recv, y_send, y_recv, s_send, s_recv,
     rx_send, rx_recv, rz_send, rz_recv, gz_send, gz_recv, gx_send, gx_recv,
@@ -85,29 +88,41 @@
         cp.wait()
     own = states_ref[...].astype(F32)
     normed = own * lax.rsqrt(jnp.mean(own * own, -1, keepdims=True) + 1e-6)
-    zbuf[pl.ds(z * OWN, OWN)] = (normed * gain_ref[...]).astype(BF16)
-    lane = lax.broadcasted_iota(jnp.int32, (8, 128), 1)
-    vec = jnp.zeros((8, 128), jnp.int32)
+    encoded = normed * gain_ref[...]
+    for i in range(OWN // 2):
+        a, b = encoded[2 * i], encoded[2 * i + 1]
+        tiles = [t[:, j * LANES:(j + 1) * LANES] for t in (a, b) for j in range(3)]
+        tiles.append(jnp.concatenate([a[:, 3 * LANES:], b[:, 3 * LANES:]], axis=1))
+        for j, tile in enumerate(tiles):
+            zbuf[z * (OWN // 2) + i, j] = tile.astype(BF16)
+    pl.semaphore_wait(barrier, len(near))
+
+    ZPARTS = OWN // 2
+
+    def z_copy(d, part, right):
+        st = 2 - d % 2
+        at = ((z - d + st + NZ) % NZ if right else (z + d - st) % NZ) * ZPARTS + part
+        ref = zbuf.at[at]
+        if right:
+            return remote(ref, ref, zr_send.at[d - 1, part], zr_recv.at[d - 1, part], to_z(st))
+        return remote(ref, ref, zl_send.at[d - 1, part], zl_recv.at[d - 1, part], to_z(-st))
+
+    chains = [(right, part) for part in range(ZPARTS) for right in (True, False)]
+    reach = {(right, part): 8 if right == (part % 2 == 0) else 7 for right, part in chains}
+    live = {}
+    def z_start(d):
+        for right, part in chains:
+            if d <= reach[right, part]:
+                live[right, part, d] = start(z_copy(d, part, right))
+
+    z_start(2)
+    z_start(1)
+
+    lane = lax.broadcasted_iota(jnp.int32, (8, LANES), 1)
+    vec = jnp.zeros((8, LANES), jnp.int32)
     for r in range(REQ):
         vec = jnp.where(lane == r, place_ref[ids_ref[r % NEIGH, r // NEIGH]], vec)
     idbuf[x] = vec
-
-    pl.semaphore_wait(barrier, len(near))
-
-    def z_copy(d, part, right):
-        st = 2 - d % 2
-        at = ((z - d + st + NZ) % NZ if right else (z + d - st) % NZ) * OWN + part * (OWN // ZPARTS)
-        ref = zbuf.at[pl.ds(at, OWN // ZPARTS)]
-        if right:
-            return remote(ref, ref, zr_send.at[d - 1, part], zr_recv.at[d - 1, part], to_z(st))
-        return remote(ref, ref, zl_send.at[d - 1, part], zl_recv.at[d - 1, part], to_z(-st))
-
-    chains = [(right, part) for part in range(ZPARTS) for right in (True, False)]
-    reach = {(right, part): 8 if right == (part % 2 == 0) else 7 for right, part in chains}
-    live = {}
-    for d in (2, 1):
-        for right, part in chains:
-            live[right, part, d] = start(z_copy(d, part, right))
     id_copies = [
         start(remote(idbuf.at[x], idbuf.at[x], id_send.at[k - 1], id_recv.at[k - 1], to_x(k)))
         for k in (2, 1, 3)
@@ -115,9 +130,9 @@
     for d in (2, 4, 6):
         for right, part in chains:
             live[right, part, d].wait_recv()
-            for e in (d + 2, d + 1):
-                if e <= reach[right, part]:
-                    live[right, part, e] = start(z_copy(e, part, right))
+            if d + 2 <= reach[right, part]:
+                live[right, part, d + 2] = start(z_copy(d + 2, part, right))
+        z_start(d + 1)
         if d == 2:
             for cp in id_copies:
                 cp.wait_recv()
@@ -128,52 +143,79 @@
         if d not in (2, 4, 6):
             cp.wait_recv()
 
+    low_half = lax.broadcasted_iota(jnp.int32, (SLICE, LANES), 1) < LANES // 2
+
     def wanted(who, r):
         p = ids_s[who, 0, r]
         return lax.rem(p, NZ * OWN), lax.div(p, NZ * OWN)
 
+    def pick_pair(who, i):
+        tiles, tails = [], []
+        for n in range(2):
+            at = wanted(who, 2 * i + n)[0]
+            pair, odd = lax.div(at, 2), lax.rem(at, 2)
+            tiles += [zbuf[pair, 3 * odd + j] for j in range(3)]
+            tail = zbuf[pair, 6].astype(F32)
+            tails.append(jnp.where(odd == n, tail, pltpu.roll(tail, LANES // 2, 1)))
+        tiles.append(jnp.where(low_half, tails[0], tails[1]).astype(BF16))
+        return tiles
+
     x_copies = {}
-    for j in range(QUARTERS):
+
+    def ask(i):
         for k in (2, 1, 3):
-            for r in range(j * QSLOTS, (j + 1) * QSLOTS):
-                out_x[k - 1, r] = zbuf[wanted((x + k) % NX, r)[0]]
-            slots = pl.ds(j * QSLOTS, QSLOTS)
-            x_copies[k, j] = start(
-                remote(
-                    out_x.at[k - 1, slots], from_x.at[k - 1, slots],
-                    x_send.at[k - 1, j], x_recv.at[k - 1, j], to_x(k),
-                )
+            for j, tile in enumerate(pick_pair((x + k) % NX, i)):
+                out_x[k - 1, i, j] = tile
+            if i >= WINDOW:
+                x_copies[k, i - WINDOW].wait_send()
+            x_copies[k, i] = remote(
+                out_x.at[k - 1, i], from_x.at[k - 1, i], x_send.at[k - 1, i], x_recv.at[k - 1, i], to_x(k)
             )
+            x_copies[k, i].start()
 
     y_copies, s_copies = {}, {}
 
-    def finish(j):
+    def finish(i):
         for k in (1, 3, 2):
-            x_copies[k, j].wait_recv()
-        for r in range(j * QSLOTS, (j + 1) * QSLOTS):
-            at, col = wanted(x, r)
-            block = zbuf[at]
+            x_copies[k, i].wait_recv()
+        cols = [wanted(x, 2 * i + n)[1] for n in range(2)]
+        for j, tile in enumerate(pick_pair(x, i)):
             for k in (1, 2, 3):
-                block = jnp.where(col == (x + NX - k) % NX, from_x[k - 1, r], block)
-            nb[mp, r] = block
-        ref = nb.at[mp, pl.ds(j * QSLOTS, QSLOTS)]
+                at = (x + NX - k) % NX
+                if j < 6:
+                    here = cols[j // 3] == at
+                else:
+                    here = jnp.where(low_half, cols[0], cols[1]) == at
+                tile = jnp.where(here, from_x[k - 1, i, j].astype(F32), tile.astype(F32)).astype(BF16)
+            nb[mp, i, j] = tile
+        ref = nb.at[mp, i]
         for k in (2, 1, 3):
-            y_copies[k, j] = start(remote(ref, ref, y_send.at[k - 1, j], y_recv.at[k - 1, j], to_y(k)))
-        s_copies[0, j] = start(remote(ref, ref, s_send.at[0, j], s_recv.at[0, j], sib))
-
-    def relay(j):
+            y_copies[k, i] = start(remote(ref, ref, y_send.at[k - 1, i], y_recv.at[k - 1, i], to_y(k)))
+        s_copies[0, i] = start(remote(ref, ref, s_send.at[0, i], s_recv.at[0, i], sib))
+
+    def relay(i):
         for k in (1, 3, 2):
-            y_copies[k, j].wait_recv()
-            ref = nb.at[(y + NY - k) % NY * 2 + c, pl.ds(j * QSLOTS, QSLOTS)]
-            s_copies[k, j] = start(remote(ref, ref, s_send.at[k, j], s_recv.at[k, j], sib))
+            y_copies[k, i].wait_recv()
+            ref = nb.at[(y + NY - k) % NY * 2 + c, i]
+            s_copies[k, i] = start(remote(ref, ref, s_send.at[k, i], s_recv.at[k, i], sib))
+
+    def rows_of_unit(u):
+        rows = NMP * SLICE
+        main = [nb[:, u, j].reshape(rows, LANES) for j in range(6)]
+        tail = nb[:, u, 6].reshape(rows, LANES).astype(F32)
+        second = pltpu.roll(tail, LANES // 2, 1)
+        ends = [t[:, :LANES // 2].astype(BF16) for t in (tail, second)]
+        return jnp.concatenate(
+            [jnp.concatenate(main[3 * n:3 * n + 3] + [ends[n]], axis=1) for n in range(2)], axis=0
+        )
 
     scale = HD ** (-0.5)
 
-    def attend(j):
-        for k in range(4):
-            s_copies[k, j].wait_recv()
-        units = range(2 * j, 2 * j + 2)
-        encs = [nb[:, NEIGH * u:NEIGH * (u + 1)].reshape(NMP * NEIGH * SLICE, DE) for u in units]
+    def attend(units):
+        for u in units:
+            for k in range(4):
+                s_copies[k, u].wait_recv()
+        encs = [rows_of_unit(u) for u in units]
         keys = [dot(e, w_ref[0], 1, 0).astype(BF16) for e in encs]
         values = [dot(e, w_ref[1], 1, 0).astype(BF16) for e in encs]
         cells = []
@@ -197,27 +239,36 @@
             dks.append(dot(ds, q, 0, 0).astype(BF16))
             dvs.append(dot(pb, g, 0, 0).astype(BF16))
         enc = jnp.concatenate(encs, axis=0)
-        dk = jnp.concatenate([jnp.concatenate(dks[0:2], axis=1), jnp.concatenate(dks[2:4], axis=1)], axis=0)
-        dv = jnp.concatenate([jnp.concatenate(dvs[0:2], axis=1), jnp.concatenate(dvs[2:4], axis=1)], axis=0)
+        dk, dv = (
+            jnp.concatenate(
+                [jnp.concatenate(d[2 * n:2 * n + 2], axis=1) for n in range(len(units))], axis=0
+            )
+            for d in (dks, dvs)
+        )
         for side, d in enumerate((dk, dv)):
             total = dot(enc, d, 0, 0)
             for h in range(2):
                 part = total[:, h * HD:(h + 1) * HD]
-                if j == 0:
+                if units[0] == 0:
                     grad[2 * side + h] = part
                 else:
                     grad[2 * side + h] += part
 
-    for step in range(QUARTERS + 2):
-        if step < QUARTERS:
-            finish(step)
-        if 0 <= step - 1 < QUARTERS:
-            relay(step - 1)
-        if step == 2:
+    for i in range(PAIRS + LAG + 3):
+        if i < PAIRS:
+            ask(i)
+        if 0 <= i - LAG < PAIRS:
+            finish(i - LAG)
+        if 0 <= i - LAG - 3 < PAIRS:
+            relay(i - LAG - 3)
+        if i == LAG + 4:
             for cp in loads[4:]:
                 cp.wait()
-        if 0 <= step - 2 < QUARTERS:
-            attend(step - 2)
+        for units in GROUPS.get(i - LAG, ()):
+            attend(units)
+    for k in (1, 2, 3):
+        for i in range(PAIRS - WINDOW, PAIRS):
+            x_copies[k, i].wait_send()
 
     stores = [
         pltpu.make_async_copy(out_ref, out_hbm, store_sem.at[0]),
@@ -226,15 +277,14 @@
     for cp in stores:
         cp.start()
 
-    HALF = DE // 2
     rx = {}
-    for half in range(2):
-        span = slice(half * HALF, (half + 1) * HALF)
-        at = pl.ds(half * HALF, HALF)
+    for i in range(NPIECE // 2):
+        span = slice(2 * i * PIECE, (2 * i + 2) * PIECE)
+        at = pl.ds(2 * i * PIECE, 2 * PIECE)
         for k in (2, 1, 3):
             xs[k - 1, span] = grad[(x + k) % NX, span].astype(BF16)
-            rx[k, half] = start(
-                remote(xs.at[k - 1, at], xr.at[k - 1, at], rx_send.at[k - 1, half], rx_recv.at[k - 1, half], to_x(k))
+            rx[k, i] = start(
+                remote(xs.at[k - 1, at], xr.at[k - 1, at], rx_send.at[k - 1, i], rx_recv.at[k - 1, i], to_x(k))
             )
 
     prod = jnp.zeros((DE, HD), F32)
@@ -256,36 +306,42 @@
     def z_out(t):
         return remote(zs.at[rows_of(t)], rbuf.at[z], rz_send.at[t], rz_recv.at[z], (x * NZ + t, mp))
 
-    def sum_x(half):
+    def sum_x(i):
         for k in (1, 3, 2):
-            rx[k, half].wait_recv()
-        span = slice(half * HALF, (half + 1) * HALF)
+            rx[k, i].wait_recv()
+        span = slice(2 * i * PIECE, (2 * i + 2) * PIECE)
         total = grad[x, span]
         for k in (1, 2, 3):
             total = total + xr[k - 1, span].astype(F32)
         acc[span] = total
         zs[span] = total.astype(BF16)
-        for t in range(half, NPIECE, 2):
+        for p in (2 * i, 2 * i + 1):
+            t = 2 * p if p < NPIECE // 2 else 2 * p + 1 - NPIECE
             pl.when(z != t)(z_out(t).start)
 
-    sum_x(0)
-    for cp in m_copies:
-        cp.wait_recv()
-    gx[x] = functools.reduce(lambda s, m: s + gm[m], range(1, NMP), gm[0])
-    h_copies = [
-        start(remote(gx.at[x], gx.at[x], h_send.at[k - 1], h_recv.at[k - 1], to_x(k))) for k in (2, 1, 3)
-    ]
-    sum_x(1)
+    for i in range(NPIECE // 2):
+        sum_x(i)
+        if i == 2:
+            for cp in m_copies:
+                cp.wait_recv()
+            gx[x] = functools.reduce(lambda s, m: s + gm[m], range(1, NMP), gm[0])
+            h_copies = [
+                start(remote(gx.at[x], gx.at[x], h_send.at[k - 1], h_recv.at[k - 1], to_x(k)))
+                for k in (2, 1, 3)
+            ]
     for cp in h_copies:
         cp.wait_recv()
     gz[z] = functools.reduce(lambda s, m: s + gx[m], range(1, NX), gx[0])
+    by_distance = sorted(range(1, NZ), key=lambda k: -min(k, NZ - k))
     v_copies = [
-        start(remote(gz.at[z], gz.at[z], v_send.at[k - 1], v_recv.at[k - 1], to_z(k)))
-        for k in range(1, NZ)
+        start(remote(gz.at[z], gz.at[z], v_send.at[k - 1], v_recv.at[k - 1], to_z(k))) for k in by_distance
     ]
 
+    def part_of(j, rows):
+        return gkv_ref.at[j // 2, rows, pl.ds(pl.multiple_of(j % 2 * HD, HD), HD)]
+
     def z_back(k):
-        ref = full.at[x, rows_of(z)]
+        ref = part_of(x, rows_of(z))
         return remote(ref, ref, gz_send.at[k - 1], gz_recv.at[z], to_z(k))
 
     @pl.when(z < NPIECE)
@@ -297,16 +353,17 @@
         total = acc[rows_of(z)]
         for s in range(NZ):
             total = total + rbuf[s].astype(F32)
-        full[x, rows_of(z)] = total.astype(BF16)
-        for k in range(1, NZ):
+        part_of(x, rows_of(z))[...] = total.astype(BF16)
+        for k in by_distance:
             z_back(k).start()
 
+    HALF = DE // 2
     back = {}
     for half in range(2):
         for t in range(half, NPIECE, 2):
-            ref = full.at[x, rows_of(t)]
+            ref = part_of(x, rows_of(t))
             pl.when(z != t)(remote(ref, ref, gz_send.at[0], gz_recv.at[t], to_z(1)).wait_recv)
-        ref = full.at[x, pl.ds(half * HALF, HALF)]
+        ref = part_of(x, pl.ds(half * HALF, HALF))
         for k in (2, 1, 3):
             back[k, half] = start(remote(ref, ref, gx_send.at[k - 1, half], gx_recv.at[k - 1, half], to_x(k)))
 
@@ -318,9 +375,6 @@
     for half in range(2):
         for k in (1, 3, 2):
             back[k, half].wait_recv()
-        span = slice(half * HALF, (half + 1) * HALF)
-        for j in range(4):
-            gkv_ref[j // 2, span, (j % 2) * HD:(j % 2 + 1) * HD] = full[j, span]
         at = pl.ds(half * HALF, HALF)
         cp = pltpu.make_async_copy(gkv_ref.at[:, at], gkv_hbm.at[:, at], store_sem.at[2 + half])
         cp.start()
@@ -371,7 +425,7 @@
 def body(queries, states, gain, w_kv, neighbour_ids, block_place, grad_out):
     dma = pltpu.SemaphoreType.DMA
     vmem = pltpu.VMEM
-    block = (SLICE, DE)
+    pair = (TILES, SLICE, LANES)
     tok, cols = queries.shape
     hbm = pl.BlockSpec(memory_space=pltpu.HBM)
     out_spec = pl.BlockSpec(memory_space=pltpu.VMEM)
@@ -398,28 +452,27 @@
             vmem((tok, cols), BF16),
             vmem(w_kv.shape, BF16),
             dma((4,)),
-            vmem((NZ * OWN,) + block, BF16),
+            vmem((NZ * OWN // 2,) + pair, BF16),
             vmem((NX, 8, 128), jnp.int32),
             pltpu.SMEM((NX, 8, 128), jnp.int32),
-            vmem((3, REQ) + block, BF16),
-            vmem((3, REQ) + block, BF16),
-            vmem((NMP, REQ) + block, BF16),
+            vmem((3, PAIRS) + pair, BF16),
+            vmem((3, PAIRS) + pair, BF16),
+            vmem((NMP, PAIRS) + pair, BF16),
             vmem((4, DE, HD), F32),
             vmem((3, DE, HD), BF16),
             vmem((3, DE, HD), BF16),
             vmem((DE, HD), F32),
             vmem((DE, HD), BF16),
             vmem((NZ, PIECE, HD), BF16),
-            vmem((NX, DE, HD), BF16),
             vmem((NMP, 1, GAIN_PAD), F32),
             vmem((NX, 1, GAIN_PAD), F32),
             vmem((NZ, 1, GAIN_PAD), F32),
             dma((3,)), dma((3,)), dma,
-            dma((8, ZPARTS)), dma((8, ZPARTS)), dma((8, ZPARTS)), dma((8, ZPARTS)),
-            dma((3, QUARTERS)), dma((3, QUARTERS)),
-            dma((3, QUARTERS)), dma((3, QUARTERS)),
-            dma((4, QUARTERS)), dma((4, QUARTERS)),
-            dma((3, 2)), dma((3, 2)), dma((NZ,)), dma((NZ,)), dma((NZ,)), dma((NZ,)),
+            dma((8, 2)), dma((8, 2)), dma((8, 2)), dma((8, 2)),
+            dma((3, PAIRS)), dma((3, PAIRS)),
+            dma((3, PAIRS)), dma((3, PAIRS)),
+            dma((4, PAIRS)), dma((4, PAIRS)),
+            dma((3, NPIECE)), dma((3, NPIECE)), dma((NZ,)), dma((NZ,)), dma((NZ,)), dma((NZ,)),
             dma((3, 2)), dma((3, 2)),
             dma((NMP,)), dma((NMP,)), dma((3,)), dma((3,)), dma((NZ,)), dma((NZ,)),
         ],

time: 89.7 us -> 86.3 us (0.962)
  Pallas kernels: 88.9 us -> 85.5 us
    pallas_call x1, Pallas kernels: 86.9 us -> 83.5 us  [body(): pl.pallas_call(kernel, out_shape=(jax.ShapeDtypeStruct((tok, cols), BF16)...]
where the time goes in v3:
time: 86.3 us; the launch traced here: 86.2 us
  Pallas kernels  85.5 us (99%)
    pallas_call x1, Pallas kernels, body(): pl.pallas_call(kernel, out_shape=(jax.ShapeDtypeStruct((tok, cols), BF16)...  83.5 us
    pallas_call x1, Pallas kernels, hand_over(): pl.pallas_call(hand_over_kernel, out_shape=tuple((jax.ShapeDtypeStruct(r....  2.02 us

profile of v3, /device:TPU:1, one launch (start us, length us, event | category | flops | bytes accessed | tf_op | source)
XLA Modules:
  0.0 86.2 jit_solution(9813360415403764944)
XLA Ops:
  0.6 83.5 %retro_step.1 = (bf16[512,256]{1,0:T(8,128)(2,1)}, bf16[512,256]{1,0:T(8,128)(2,1)}, bf16[2,448,256]{2,1,0:T(8,128)(2,1)}, f32[1,448]{1,0:T(1,128)}) custom-call(bf16[4,16,448]{2,1,0:T(8,128)(2,1)} %states_hbm.1, f32[1,448]{1,0:T(1,128)} %bitcast.3, s32[2,8]{1,0:T(2,128)} %bitcast.4, s32[256]{0:T(256)} %place_hbm.1, bf16[2,448,256]{2,1,0:T(8,128)(2,1)} %w_hbm.1, ...), custom_call_target="tpu_custom_call" | custom-call | tf_op jit(solution)/shard_map/retro_step/pallas_call | solution.py:432
  84.2 2.0 %hand_over.1 = (bf16[512,256]{1,0:T(8,128)(2,1)}, bf16[512,256]{1,0:T(8,128)(2,1)}, bf16[2,448,256]{2,1,0:T(8,128)(2,1)}, f32[1,448]{1,0:T(1,128)}) custom-call(bf16[512,256]{1,0:T(8,128)(2,1)} %get-tuple-element.12.refs_0_, bf16[512,256]{1,0:T(8,128)(2,1)} %get-tuple-element.13.refs_1_, bf16[2,448,256]{2,1,0:T(8,128)(2,1)} %get-tuple-element.14.refs_2_, ...), custom_call_target="tpu_custom_call" | custom-call | tf_op jit(solution)/shard_map/hand_over/pallas_call | solution.py:414

commit v4 on v3

--- a/solution.py
+++ b/solution.py
@@ -22,8 +22,9 @@
 NPIECE = DE // PIECE
 PAIRS = REQ // 2
 TILES = 7
-WINDOW = 2
-LAG = 3
+ODD_AFTER = {0: (), 2: (1,), 4: (3, 5), 6: (7,)}
+WINDOW = 3
+LAG = 4
 GROUPS = {7: ((0, 1, 2, 3),), 10: ((4, 5, 6, 7),)}
 LANES = 128
 F32 = jnp.float32
@@ -47,7 +48,7 @@
     states_ref, gain_ref, ids_ref, place_ref, w_ref, q_ref, g_ref, load_sem,
     out_ref, dq_ref, gkv_ref, store_sem,
     zbuf, idbuf, ids_s, out_x, from_x, nb,
-    grad, xs, xr, acc, zs, rbuf, gm, gx, gz,
+    grad, xs, xr, acc, zs, rbuf, full, gm, gx, gz,
     id_send, id_recv, id_local, zr_send, zr_recv, zl_send, zl_recv,
     x_send, x_recv, y_send, y_recv, s_send, s_recv,
     rx_send, rx_recv, rz_send, rz_recv, gz_send, gz_recv, gx_send, gx_recv,
@@ -116,7 +117,8 @@
                 live[right, part, d] = start(z_copy(d, part, right))
 
     z_start(2)
-    z_start(1)
+    for d in ODD_AFTER[0]:
+        z_start(d)
 
     lane = lax.broadcasted_iota(jnp.int32, (8, LANES), 1)
     vec = jnp.zeros((8, LANES), jnp.int32)
@@ -132,7 +134,8 @@
             live[right, part, d].wait_recv()
             if d + 2 <= reach[right, part]:
                 live[right, part, d + 2] = start(z_copy(d + 2, part, right))
-        z_start(d + 1)
+        for e in ODD_AFTER[d]:
+            z_start(e)
         if d == 2:
             for cp in id_copies:
                 cp.wait_recv()
@@ -277,15 +280,23 @@
     for cp in stores:
         cp.start()
 
-    rx = {}
-    for i in range(NPIECE // 2):
-        span = slice(2 * i * PIECE, (2 * i + 2) * PIECE)
-        at = pl.ds(2 * i * PIECE, 2 * PIECE)
-        for k in (2, 1, 3):
-            xs[k - 1, span] = grad[(x + k) % NX, span].astype(BF16)
-            rx[k, i] = start(
-                remote(xs.at[k - 1, at], xr.at[k - 1, at], rx_send.at[k - 1, i], rx_recv.at[k - 1, i], to_x(k))
-            )
+    def rows_of(t):
+        return pl.ds(pl.multiple_of((t // 2 + NPIECE // 2 * (t % 2)) * PIECE, PIECE), PIECE)
+
+    by_distance = sorted(range(1, NZ), key=lambda k: -min(k, NZ - k))
+
+    def x_out(k, t):
+        src, dst = xs.at[k - 1, rows_of(t)], xr.at[k - 1, rows_of(t)]
+        return remote(src, dst, rx_send.at[k - 1, t], rx_recv.at[k - 1, t], to_x(k))
+
+    for d in by_distance + [0]:
+        t = (z + d) % NZ
+
+        @pl.when(t < NPIECE)
+        def _():
+            for k in (2, 1, 3):
+                xs[k - 1, rows_of(t)] = grad[(x + k) % NX, rows_of(t)].astype(BF16)
+                x_out(k, t).start()
 
     prod = jnp.zeros((DE, HD), F32)
     for j in range(4):
@@ -300,28 +311,26 @@
         for k in range(1, NMP)
     ]
 
-    def rows_of(t):
-        return pl.ds(pl.multiple_of((t // 2 + NPIECE // 2 * (t % 2)) * PIECE, PIECE), PIECE)
-
     def z_out(t):
         return remote(zs.at[rows_of(t)], rbuf.at[z], rz_send.at[t], rz_recv.at[z], (x * NZ + t, mp))
 
-    def sum_x(i):
-        for k in (1, 3, 2):
-            rx[k, i].wait_recv()
-        span = slice(2 * i * PIECE, (2 * i + 2) * PIECE)
-        total = grad[x, span]
-        for k in (1, 2, 3):
-            total = total + xr[k - 1, span].astype(F32)
-        acc[span] = total
-        zs[span] = total.astype(BF16)
-        for p in (2 * i, 2 * i + 1):
-            t = 2 * p if p < NPIECE // 2 else 2 * p + 1 - NPIECE
-            pl.when(z != t)(z_out(t).start)
-
-    for i in range(NPIECE // 2):
-        sum_x(i)
-        if i == 2:
+    for n, d in enumerate(by_distance + [0]):
+        t = (z + d) % NZ
+
+        @pl.when(t < NPIECE)
+        def _():
+            for k in (1, 3, 2):
+                x_out(k, t).wait_recv()
+            total = grad[x, rows_of(t)]
+            for k in (1, 2, 3):
+                total = total + xr[k - 1, rows_of(t)].astype(F32)
+            if d == 0:
+                acc[...] = total
+            else:
+                zs[rows_of(t)] = total.astype(BF16)
+                z_out(t).start()
+
+        if n == 7:
             for cp in m_copies:
                 cp.wait_recv()
             gx[x] = functools.reduce(lambda s, m: s + gm[m], range(1, NMP), gm[0])
@@ -332,13 +341,12 @@
     for cp in h_copies:
         cp.wait_recv()
     gz[z] = functools.reduce(lambda s, m: s + gx[m], range(1, NX), gx[0])
-    by_distance = sorted(range(1, NZ), key=lambda k: -min(k, NZ - k))
     v_copies = [
         start(remote(gz.at[z], gz.at[z], v_send.at[k - 1], v_recv.at[k - 1], to_z(k))) for k in by_distance
     ]
 
     def part_of(j, rows):
-        return gkv_ref.at[j // 2, rows, pl.ds(pl.multiple_of(j % 2 * HD, HD), HD)]
+        return full.at[j, rows]
 
     def z_back(k):
         ref = part_of(x, rows_of(z))
@@ -350,7 +358,7 @@
         for s in range(NZ):
             arrival = remote(zs.at[rows_of(0)], rbuf.at[s], rz_send.at[s], rz_recv.at[s], to_z(1))
             pl.when(z != s)(arrival.wait_recv)
-        total = acc[rows_of(z)]
+        total = acc[...]
         for s in range(NZ):
             total = total + rbuf[s].astype(F32)
         part_of(x, rows_of(z))[...] = total.astype(BF16)
@@ -375,6 +383,9 @@
     for half in range(2):
         for k in (1, 3, 2):
             back[k, half].wait_recv()
+        span = slice(half * HALF, (half + 1) * HALF)
+        for j in range(4):
+            gkv_ref[j // 2, span, (j % 2) * HD:(j % 2 + 1) * HD] = full[j, span]
         at = pl.ds(half * HALF, HALF)
         cp = pltpu.make_async_copy(gkv_ref.at[:, at], gkv_hbm.at[:, at], store_sem.at[2 + half])
         cp.start()
@@ -382,6 +393,8 @@
 
     for t in range(NPIECE):
         pl.when(z != t)(z_out(t).wait_send)
+        for k in (1, 2, 3):
+            x_out(k, t).wait_send()
 
     @pl.when(z < NPIECE)
     def _():
@@ -461,9 +474,10 @@
             vmem((4, DE, HD), F32),
             vmem((3, DE, HD), BF16),
             vmem((3, DE, HD), BF16),
-            vmem((DE, HD), F32),
+            vmem((PIECE, HD), F32),
             vmem((DE, HD), BF16),
             vmem((NZ, PIECE, HD), BF16),
+            vmem((NX, DE, HD), BF16),
             vmem((NMP, 1, GAIN_PAD), F32),
             vmem((NX, 1, GAIN_PAD), F32),
             vmem((NZ, 1, GAIN_PAD), F32),

time: 86.3 us -> 85 us (0.985); the launches traced: 86.2 us -> 84 us
  Pallas kernels: 85.5 us -> 83.4 us
    pallas_call x1, Pallas kernels: 83.5 us -> 81.3 us  [body(): pl.pallas_call(kernel, out_shape=(jax.ShapeDtypeStruct((tok, cols), BF16)...]
where the time goes in v4:
time: 85 us; the launch traced here: 84 us
  Pallas kernels  83.4 us (98%)
    pallas_call x1, Pallas kernels, body(): pl.pallas_call(kernel, out_shape=(jax.ShapeDtypeStruct((tok, cols), BF16)...  81.3 us
    pallas_call x1, Pallas kernels, hand_over(): pl.pallas_call(hand_over_kernel, out_shape=tuple((jax.ShapeDtypeStruct(r....  2.02 us

profile of v4, /device:TPU:1, one launch (start us, length us, event | category | flops | bytes accessed | tf_op | source)
XLA Modules:
  0.0 84.0 jit_solution(13569805954348245004)
XLA Ops:
  0.6 81.3 %retro_step.1 = (bf16[512,256]{1,0:T(8,128)(2,1)}, bf16[512,256]{1,0:T(8,128)(2,1)}, bf16[2,448,256]{2,1,0:T(8,128)(2,1)}, f32[1,448]{1,0:T(1,128)}) custom-call(bf16[4,16,448]{2,1,0:T(8,128)(2,1)} %states_hbm.1, f32[1,448]{1,0:T(1,128)} %bitcast.3, s32[2,8]{1,0:T(2,128)} %bitcast.4, s32[256]{0:T(256)} %place_hbm.1, bf16[2,448,256]{2,1,0:T(8,128)(2,1)} %w_hbm.1, ...), custom_call_target="tpu_custom_call" | custom-call | tf_op jit(solution)/shard_map/retro_step/pallas_call | solution.py:445
  82.0 2.0 %hand_over.1 = (bf16[512,256]{1,0:T(8,128)(2,1)}, bf16[512,256]{1,0:T(8,128)(2,1)}, bf16[2,448,256]{2,1,0:T(8,128)(2,1)}, f32[1,448]{1,0:T(1,128)}) custom-call(bf16[512,256]{1,0:T(8,128)(2,1)} %get-tuple-element.12.refs_0_, bf16[512,256]{1,0:T(8,128)(2,1)} %get-tuple-element.13.refs_1_, bf16[2,448,256]{2,1,0:T(8,128)(2,1)} %get-tuple-element.14.refs_2_, ...), custom_call_target="tpu_custom_call" | custom-call | tf_op jit(solution)/shard_map/hand_over/pallas_call | solution.py:427

commit v5 on v4

--- a/solution.py
+++ b/solution.py
@@ -23,7 +23,7 @@
 PAIRS = REQ // 2
 TILES = 7
 ODD_AFTER = {0: (), 2: (1,), 4: (3, 5), 6: (7,)}
-WINDOW = 3
+WINDOW = 4
 LAG = 4
 GROUPS = {7: ((0, 1, 2, 3),), 10: ((4, 5, 6, 7),)}
 LANES = 128
@@ -166,7 +166,7 @@
     x_copies = {}
 
     def ask(i):
-        for k in (2, 1, 3):
+        for k in ((2, 1, 3) if i % 2 == 0 else (3, 1, 2)):
             for j, tile in enumerate(pick_pair((x + k) % NX, i)):
                 out_x[k - 1, i, j] = tile
             if i >= WINDOW:

time: 85 us -> 84.9 us (level)
  no operation moved by 1% of the time
where the time goes in v5:
time: 84.9 us; the launch traced here: 83.3 us
  Pallas kernels  82.7 us (97%)
    pallas_call x1, Pallas kernels, body(): pl.pallas_call(kernel, out_shape=(jax.ShapeDtypeStruct((tok, cols), BF16)...  80.6 us
    pallas_call x1, Pallas kernels, hand_over(): pl.pallas_call(hand_over_kernel, out_shape=tuple((jax.ShapeDtypeStruct(r....  2.02 us

profile of v5, /device:TPU:1, one launch (start us, length us, event | category | flops | bytes accessed | tf_op | source)
XLA Modules:
  0.0 83.3 jit_solution(14183009031668035853)
XLA Ops:
  0.6 80.6 %retro_step.1 = (bf16[512,256]{1,0:T(8,128)(2,1)}, bf16[512,256]{1,0:T(8,128)(2,1)}, bf16[2,448,256]{2,1,0:T(8,128)(2,1)}, f32[1,448]{1,0:T(1,128)}) custom-call(bf16[4,16,448]{2,1,0:T(8,128)(2,1)} %states_hbm.1, f32[1,448]{1,0:T(1,128)} %bitcast.3, s32[2,8]{1,0:T(2,128)} %bitcast.4, s32[256]{0:T(256)} %place_hbm.1, bf16[2,448,256]{2,1,0:T(8,128)(2,1)} %w_hbm.1, ...), custom_call_target="tpu_custom_call" | custom-call | tf_op jit(solution)/shard_map/retro_step/pallas_call | solution.py:445
  81.3 2.0 %hand_over.1 = (bf16[512,256]{1,0:T(8,128)(2,1)}, bf16[512,256]{1,0:T(8,128)(2,1)}, bf16[2,448,256]{2,1,0:T(8,128)(2,1)}, f32[1,448]{1,0:T(1,128)}) custom-call(bf16[512,256]{1,0:T(8,128)(2,1)} %get-tuple-element.12.refs_0_, bf16[512,256]{1,0:T(8,128)(2,1)} %get-tuple-element.13.refs_1_, bf16[2,448,256]{2,1,0:T(8,128)(2,1)} %get-tuple-element.14.refs_2_, ...), custom_call_target="tpu_custom_call" | custom-call | tf_op jit(solution)/shard_map/hand_over/pallas_call | solution.py:427
